TPU v7x, 32 devices: a whole 2x2x4 slice. The times are simulated.
32 devices in a mesh: seq: 4 (over y, x), grp: 8 (over z, core).
Axes of the slice: x: 2, y: 2, z: 4, core: 2. Of those that a mesh axis runs over, the one named last changes fastest.
Arguments:
- tokens: bfloat16 [8, 4608, 512], P('grp', 'seq'), may hold values from -6 to 6
- cotangent: bfloat16 [8, 4608, 512], P('grp', 'seq'), may hold values from -6 to 6
- lengths: int32 [8], P('grp'), may hold values from 3457 to 4608, as said below
- weight_query: float32 [512, 512], P(('seq', 'grp')), may hold values from -0.25 to 0.25
- weight_memory: float32 [3, 512, 1024], P(None, ('seq', 'grp')), may hold values from -0.15625 to 0.15625
- weight_out: float32 [512, 512], P(('seq', 'grp')), may hold values from -1.5 to 1.5
- weight_up: float32 [512, 2048], P(('seq', 'grp')), may hold values from -0.25 to 0.25
- weight_down: float32 [2048, 512], P(('seq', 'grp')), may hold values from -0.125 to 0.125
- vectors: float32 [9, 512], P(None, ('seq', 'grp')), may hold values from -0.5 to 1.5, as said below
- first_query: float32 [512, 512], P(('seq', 'grp')), may hold values from -64 to 64
- first_memory: float32 [3, 512, 1024], P(None, ('seq', 'grp')), may hold values from -40 to 40
- first_out: float32 [512, 512], P(('seq', 'grp')), may hold values from -24 to 24
- first_up: float32 [512, 2048], P(('seq', 'grp')), may hold values from -40 to 40
- first_down: float32 [2048, 512], P(('seq', 'grp')), may hold values from -80 to 80
- first_vectors: float32 [9, 512], P(None, ('seq', 'grp')), may hold values from -128 to 128
- second_query: float32 [512, 512], P(('seq', 'grp')), may hold values from 484.7616 to 1939.0464
- second_memory: float32 [3, 512, 1024], P(None, ('seq', 'grp')), may hold values from 174.36671 to 696.7296
- second_out: float32 [512, 512], P(('seq', 'grp')), may hold values from 77.4144 to 309.6576
- second_up: float32 [512, 2048], P(('seq', 'grp')), may hold values from 174.36671 to 696.7296
- second_down: float32 [2048, 512], P(('seq', 'grp')), may hold values from 696.7296 to 2790.6047
- second_vectors: float32 [9, 512], P(None, ('seq', 'grp')), may hold values from 1939.0464 to 7741.44
Outputs:
- out_tokens: bfloat16 [8, 4608, 512], P('grp', 'seq')
- grad_tokens: bfloat16 [8, 4608, 512], P('grp', 'seq')
- moment_query: float32 [512, 512], P(('seq', 'grp'))
- moment_memory: float32 [3, 512, 1024], P(None, ('seq', 'grp'))
- moment_out: float32 [512, 512], P(('seq', 'grp'))
- moment_up: float32 [512, 2048], P(('seq', 'grp'))
- moment_down: float32 [2048, 512], P(('seq', 'grp'))
- moment_vectors: float32 [9, 512], P(None, ('seq', 'grp'))
- square_query: float32 [512, 512], P(('seq', 'grp'))
- square_memory: float32 [3, 512, 1024], P(None, ('seq', 'grp'))
- square_out: float32 [512, 512], P(('seq', 'grp'))
- square_up: float32 [512, 2048], P(('seq', 'grp'))
- square_down: float32 [2048, 512], P(('seq', 'grp'))
- square_vectors: float32 [9, 512], P(None, ('seq', 'grp'))
- master_query: float32 [512, 512], P(('seq', 'grp'))
- master_memory: float32 [3, 512, 1024], P(None, ('seq', 'grp'))
- master_out: float32 [512, 512], P(('seq', 'grp'))
- master_up: float32 [512, 2048], P(('seq', 'grp'))
- master_down: float32 [2048, 512], P(('seq', 'grp'))
- master_vectors: float32 [9, 512], P(None, ('seq', 'grp'))
- copy_query: bfloat16 [512, 512], P(('seq', 'grp'))
- copy_memory: bfloat16 [3, 512, 1024], P(None, ('seq', 'grp'))
- copy_out: bfloat16 [512, 512], P(('seq', 'grp'))
- copy_up: bfloat16 [512, 2048], P(('seq', 'grp'))
- copy_down: bfloat16 [2048, 512], P(('seq', 'grp'))
- copy_vectors: bfloat16 [9, 512], P(None, ('seq', 'grp'))
Inputs may be any that keep to these rules, and one draw needn't show every extreme that they name: `lengths`: every sequence has more than 3456 live positions; some sequence fills all 4608. `vectors`: rows 0 and 2 lie between 0.5 and 1.5, the other rows between -0.5 and 0.5.
All inputs are finite; a program needn't handle non-finite values.
Results may differ from a plain program's by a relative error of at most 0.012.
The roundings to bfloat16 on the way count: a program that leaves them out, or rounds other values in their place, can miss the bound.
Values may be sent and summed in bfloat16 or wider, within the bound.
A program may use at most 128 MiB of HBM per device.

v0:
```python
import functools

import jax
import jax.numpy as jnp
from jax import lax
from jax.experimental import pallas as pl
from jax.experimental.pallas import tpu as pltpu
from jax.sharding import PartitionSpec as P

H = 8
STEP = 10


NORM_EPSILON = 1e-05
BETA_FIRST = 0.9
BETA_SECOND = 0.95
ADAM_EPSILON = 1e-08
WEIGHT_DECAY = 0.1
LEARNING_RATES = (0.05, 0.04, 0.3, 0.05, 0.03, 0.5)
MASKED_SCORE = -1e30
NT = (((1,), (1,)), ((), ()))


def from_behind(x, axis, by):
    peers = lax.axis_size(axis)
    pairs = [(i, i + by) for i in range(peers) if 0 <= i + by < peers]
    return lax.ppermute(x, axis, pairs)


def matmul(left, right):
    return jnp.dot(left, right, preferred_element_type=jnp.float32)


def over_rows(left, right):
    return lax.dot_general(
        left, right, (((0,), (0,)), ((), ())), preferred_element_type=jnp.float32
    )


def against(left, right):
    return lax.dot_general(
        left, right, (((1,), (1,)), ((), ())), preferred_element_type=jnp.float32
    )


def norm_forward(values, gain, shift):
    centred = values - jnp.mean(values, axis=-1, keepdims=True)
    factor = lax.rsqrt(jnp.mean(centred * centred, axis=-1, keepdims=True) + NORM_EPSILON)
    unit_rows = centred * factor
    return (unit_rows * gain + shift, unit_rows, factor)


def norm_backward(upstream, unit_rows, factor, gain):
    scaled = upstream * gain
    inward = factor * (
        scaled
        - jnp.mean(scaled, axis=-1, keepdims=True)
        - unit_rows * jnp.mean(scaled * unit_rows, axis=-1, keepdims=True)
    )
    return (inward, jnp.sum(upstream * unit_rows, axis=0), jnp.sum(upstream, axis=0))


def masked_scores(query_tile_rows, key_row_block, positions):
    slot_starts = 3 * jnp.arange(key_row_block.shape[0], dtype=jnp.int32)
    score_matrix = jnp.einsum(
        "azv,lzv->zal", query_tile_rows, key_row_block, preferred_element_type=jnp.float32
    ) * query_tile_rows.shape[2] ** (-0.5)
    visible = slot_starts[None, :] <= positions[:, None]
    return jnp.where(visible[None], score_matrix, MASKED_SCORE)


def attend_forward(queries, key_row_block, value_row_block, anchor, block_rows):
    block_count = queries.shape[0] // block_rows
    offsets = block_rows * jnp.arange(block_count, dtype=jnp.int32)

    def attend_block(inputs):
        query_tile_rows, offset_rows = inputs
        score_matrix = masked_scores(
            query_tile_rows,
            key_row_block,
            anchor + offset_rows + jnp.arange(block_rows, dtype=jnp.int32),
        )
        highest = jnp.max(score_matrix, axis=-1, keepdims=True)
        exponent = jnp.exp(score_matrix - highest)
        summed = jnp.sum(exponent, axis=-1, keepdims=True)
        reduced_weights = (exponent / summed).astype(jnp.bfloat16)
        mixed = jnp.einsum(
            "yup,pyb->uyb", reduced_weights, value_row_block, preferred_element_type=jnp.float32
        )
        return (mixed, (highest + jnp.log(summed))[..., 0])

    blocks_in = queries.reshape(block_count, block_rows, queries.shape[1], queries.shape[2])
    mixed, logsum = lax.map(attend_block, (blocks_in, offsets))
    return (mixed.reshape(queries.shape), logsum)


def attend_backward(queries, key_row_block, value_row_block, upstream, logsum, anchor, block_rows):
    block_count = queries.shape[0] // block_rows
    offsets = block_rows * jnp.arange(block_count, dtype=jnp.int32)
    scale_factor = queries.shape[2] ** (-0.5)

    def attend_back(carry, inputs):
        grad_keys, grad_values = carry
        query_tile_rows, incoming_gradient_rows, logsum_block, offset_rows = inputs
        score_matrix = masked_scores(
            query_tile_rows,
            key_row_block,
            anchor + offset_rows + jnp.arange(block_rows, dtype=jnp.int32),
        )
        weights_soft = jnp.exp(score_matrix - logsum_block[..., None])
        grad_weights = jnp.einsum(
            "azv,lzv->zal",
            incoming_gradient_rows,
            value_row_block,
            preferred_element_type=jnp.float32,
        )
        centre = jnp.sum(weights_soft * grad_weights, axis=-1, keepdims=True)
        score_gradient = (weights_soft * (grad_weights - centre)).astype(jnp.bfloat16)
        grad_query = (
            jnp.einsum(
                "yup,pyb->uyb", score_gradient, key_row_block, preferred_element_type=jnp.float32
            )
            * scale_factor
        )
        grad_keys = (
            grad_keys
            + jnp.einsum(
                "xof,oxa->fxa", score_gradient, query_tile_rows, preferred_element_type=jnp.float32
            )
            * scale_factor
        )
        grad_values = grad_values + jnp.einsum(
            "xof,oxa->fxa",
            weights_soft.astype(jnp.bfloat16),
            incoming_gradient_rows,
            preferred_element_type=jnp.float32,
        )
        return ((grad_keys, grad_values), grad_query)

    shape_blocks = (block_count, block_rows, queries.shape[1], queries.shape[2])
    zeros_init = jnp.zeros(key_row_block.shape, jnp.float32)
    (grad_keys, grad_values), grad_query = lax.scan(
        attend_back,
        (zeros_init, zeros_init),
        (queries.reshape(shape_blocks), upstream.reshape(shape_blocks), logsum, offsets),
    )
    return (grad_query.reshape(queries.shape), grad_keys, grad_values)


def adamw(weight, gradient, moment, square, step_rate):
    moment_new = BETA_FIRST * moment + (1.0 - BETA_FIRST) * gradient
    square_new = BETA_SECOND * square + (1.0 - BETA_SECOND) * gradient * gradient
    fixed_first = 1.0 - BETA_FIRST**STEP
    fixed_second = 1.0 - BETA_SECOND**STEP
    update = (
        moment_new / fixed_first / (jnp.sqrt(square_new / fixed_second) + ADAM_EPSILON)
        + WEIGHT_DECAY * weight
    )
    master = weight - step_rate * update
    return (moment_new, square_new, master, master.astype(jnp.bfloat16))


def plain(
    tokens,
    cotangent,
    lengths,
    weight_query,
    weight_memory,
    weight_out,
    weight_up,
    weight_down,
    vectors,
    first_query,
    first_memory,
    first_out,
    first_up,
    first_down,
    first_vectors,
    second_query,
    second_memory,
    second_out,
    second_up,
    second_down,
    second_vectors,
):
    gathered = (
        lax.all_gather(weight_query.astype(jnp.bfloat16), ("seq", "grp"), axis=0, tiled=True),
        lax.all_gather(weight_memory.astype(jnp.bfloat16), ("seq", "grp"), axis=1, tiled=True),
        lax.all_gather(weight_out.astype(jnp.bfloat16), ("seq", "grp"), axis=0, tiled=True),
        lax.all_gather(weight_up.astype(jnp.bfloat16), ("seq", "grp"), axis=0, tiled=True),
        lax.all_gather(weight_down.astype(jnp.bfloat16), ("seq", "grp"), axis=0, tiled=True),
        lax.all_gather(vectors.astype(jnp.bfloat16), ("seq", "grp"), axis=1, tiled=True),
    )
    query_w, memory_w, out_w, up_w, down_w, vector_low = gathered
    vector_rows = vector_low.astype(jnp.float32)
    model_width = query_w.shape[0]
    hidden_units = up_w.shape[1]
    head_size = model_width // H
    seq_count = lax.axis_size("seq")
    seq_index = lax.axis_index("seq")
    local_rows = tokens.shape[1]
    local_slots = local_rows // 3
    inputs = tokens[0].astype(jnp.float32)
    normed, unit_one, factor_one = norm_forward(inputs, vector_rows[0], vector_rows[1])
    normed_low = normed.astype(jnp.bfloat16)
    queries = matmul(normed_low, query_w).astype(jnp.bfloat16)
    borrowed = from_behind(normed_low[local_rows - 2 :], "seq", 1)
    extended = jnp.concatenate([borrowed, normed_low], axis=0)
    windows = extended[:local_rows].reshape(local_slots, 3 * model_width)
    memory_flat = memory_w.reshape(3 * model_width, 2 * model_width)
    memory = matmul(windows, memory_flat).astype(jnp.bfloat16)
    share_width = model_width // seq_count
    local_heads = H // seq_count
    head_queries, head_memory = (
        lax.all_to_all(
            queries.reshape(local_rows, 1, seq_count, share_width),
            "seq",
            split_axis=2,
            concat_axis=0,
            tiled=True,
        ),
        lax.all_to_all(
            memory.reshape(local_slots, 2, seq_count, share_width),
            "seq",
            split_axis=2,
            concat_axis=0,
            tiled=True,
        ),
    )
    total_rows = head_queries.shape[0]
    total_slots = head_memory.shape[0]
    query_heads = head_queries.reshape(total_rows, local_heads, head_size)
    key_heads = head_memory[:, 0].reshape(total_slots, local_heads, head_size)
    value_heads = head_memory[:, 1].reshape(total_slots, local_heads, head_size)
    block_rows = min(512, total_rows)
    mixed, logsum = attend_forward(query_heads, key_heads, value_heads, 0, block_rows)
    mixed_low = mixed.astype(jnp.bfloat16).reshape(total_rows, 1, share_width)
    attended = lax.all_to_all(mixed_low, "seq", split_axis=0, concat_axis=1, tiled=True).reshape(
        local_rows, model_width
    )
    residual = inputs + matmul(attended, out_w)
    normed_two, unit_two, factor_two = norm_forward(residual, vector_rows[2], vector_rows[3])
    normed_two_low = normed_two.astype(jnp.bfloat16)
    pre_act = matmul(normed_two_low, up_w) + vector_rows[5:].reshape(hidden_units)
    activated, gelu_pull = jax.vjp(jax.nn.gelu, pre_act)
    activated_low = activated.astype(jnp.bfloat16)
    result = residual + matmul(activated_low, down_w) + vector_rows[4]
    positions = seq_index * local_rows + jnp.arange(local_rows, dtype=jnp.int32)
    live_mask = (positions < lengths[0]).astype(jnp.float32)
    grad_out = cotangent[0].astype(jnp.float32) * live_mask[:, None]
    grad_out_low = grad_out.astype(jnp.bfloat16)
    grad_down = over_rows(activated_low, grad_out_low)
    grad_activated = against(grad_out_low, down_w)
    grad_pre_low = gelu_pull(grad_activated)[0].astype(jnp.bfloat16)
    grad_up = over_rows(normed_two_low, grad_pre_low)
    grad_up_bias = jnp.sum(grad_pre_low.astype(jnp.float32), axis=0)
    grad_normed_two = against(grad_pre_low, up_w)
    grad_norm_two, grad_gain_two, grad_shift_two = norm_backward(
        grad_normed_two, unit_two, factor_two, vector_rows[2]
    )
    grad_residual = grad_out + grad_norm_two
    grad_branch_low = grad_residual.astype(jnp.bfloat16)
    grad_outw = over_rows(attended, grad_branch_low)
    grad_attended_low = against(grad_branch_low, out_w).astype(jnp.bfloat16)
    grad_heads = lax.all_to_all(
        grad_attended_low.reshape(local_rows, 1, seq_count, share_width),
        "seq",
        split_axis=2,
        concat_axis=0,
        tiled=True,
    ).reshape(total_rows, local_heads, head_size)
    grad_q, grad_k, grad_v = attend_backward(
        query_heads, key_heads, value_heads, grad_heads, logsum, 0, block_rows
    )
    packed = (
        jnp.stack([grad_k, grad_v], axis=1)
        .astype(jnp.bfloat16)
        .reshape(total_slots, 2, 1, share_width)
    )
    token_queries, token_memory = (
        lax.all_to_all(
            grad_q.astype(jnp.bfloat16).reshape(total_rows, 1, 1, share_width),
            "seq",
            split_axis=0,
            concat_axis=2,
            tiled=True,
        ),
        lax.all_to_all(packed, "seq", split_axis=0, concat_axis=2, tiled=True),
    )
    grad_queries_low = token_queries.reshape(local_rows, model_width)
    grad_memory_low = token_memory.reshape(local_slots, 2 * model_width)
    grad_queryw = over_rows(normed_low, grad_queries_low)
    grad_normed = against(grad_queries_low, query_w)
    grad_memoryw = over_rows(windows, grad_memory_low).reshape(3, model_width, 2 * model_width)
    grad_windows = against(grad_memory_low, memory_flat).reshape(local_rows, model_width)
    returned = from_behind(grad_windows[:2], "seq", -1)
    grad_normed = grad_normed + jnp.concatenate([grad_windows[2:], returned], axis=0)
    grad_norm_one, grad_gain_one, grad_shift_one = norm_backward(
        grad_normed, unit_one, factor_one, vector_rows[0]
    )
    grad_inputs = (grad_residual + grad_norm_one).astype(jnp.bfloat16)
    grad_vector_rows = jnp.concatenate(
        [
            jnp.stack(
                [
                    grad_gain_one,
                    grad_shift_one,
                    grad_gain_two,
                    grad_shift_two,
                    jnp.sum(grad_out, axis=0),
                ]
            ),
            grad_up_bias.reshape(4, model_width),
        ],
        axis=0,
    )
    reduced = (
        lax.psum_scatter(grad_queryw, ("seq", "grp"), scatter_dimension=0, tiled=True),
        lax.psum_scatter(grad_memoryw, ("seq", "grp"), scatter_dimension=1, tiled=True),
        lax.psum_scatter(grad_outw, ("seq", "grp"), scatter_dimension=0, tiled=True),
        lax.psum_scatter(grad_up, ("seq", "grp"), scatter_dimension=0, tiled=True),
        lax.psum_scatter(grad_down, ("seq", "grp"), scatter_dimension=0, tiled=True),
        lax.psum_scatter(grad_vector_rows, ("seq", "grp"), scatter_dimension=1, tiled=True),
    )
    new_query = adamw(weight_query, reduced[0], first_query, second_query, LEARNING_RATES[0])
    new_memory = adamw(weight_memory, reduced[1], first_memory, second_memory, LEARNING_RATES[1])
    new_out = adamw(weight_out, reduced[2], first_out, second_out, LEARNING_RATES[2])
    new_up = adamw(weight_up, reduced[3], first_up, second_up, LEARNING_RATES[3])
    new_down = adamw(weight_down, reduced[4], first_down, second_down, LEARNING_RATES[4])
    new_vectors = adamw(vectors, reduced[5], first_vectors, second_vectors, LEARNING_RATES[5])
    return (
        result.astype(jnp.bfloat16)[None],
        grad_inputs[None],
        new_query[0],
        new_memory[0],
        new_out[0],
        new_up[0],
        new_down[0],
        new_vectors[0],
        new_query[1],
        new_memory[1],
        new_out[1],
        new_up[1],
        new_down[1],
        new_vectors[1],
        new_query[2],
        new_memory[2],
        new_out[2],
        new_up[2],
        new_down[2],
        new_vectors[2],
        new_query[3],
        new_memory[3],
        new_out[3],
        new_up[3],
        new_down[3],
        new_vectors[3],
    )


MESH = pl.DeviceIdType.MESH
LOW, WIDE = jnp.bfloat16, jnp.float32
ROWS = 16
PART = 384
STRIP = 2 * PART
SLOTS = STRIP // 3
EARLY = 7
LATE = 5
MEGA = 1024 * 1024
SCATTER_ORDERS = ("yzx", "xyz", "zxy", "xyz", "sz", "xyz", "yzx", "sz", "sz")


def in_vmem(count):
    return [pl.BlockSpec(memory_space=pltpu.VMEM)] * count


def shaped(*shape, kind=jnp.bfloat16):
    return jax.ShapeDtypeStruct(shape, kind)


def dot(left, right):
    return jnp.dot(left, right, preferred_element_type=jnp.float32)


def differ(bit, other):
    return bit + other - 2 * bit * other


class Place:
    def __init__(self, depth):
        self.seq, self.grp = lax.axis_index("seq"), lax.axis_index("grp")
        self.depth = depth
        self.y, self.x = lax.div(self.seq, 2), lax.rem(self.seq, 2)
        self.z, self.c = lax.div(self.grp, 2), lax.rem(self.grp, 2)
        self.own = {"y": self.y, "x": self.x, "z": self.z, "s": self.seq}
        self.size = {"y": 2, "x": 2, "z": depth, "s": 4}

    def turn_to(self, shard):
        return 2 * differ(self.y, lax.div(shard, 2)) + differ(self.x, lax.rem(shard, 2))

    def strip(self, it):
        half, pos = differ(lax.div(it, 3), self.y), lax.rem(it, 3)
        return 3 * half + pos + self.x * (2 - 2 * pos)

    def shard(self, turn):
        return 2 * differ(self.y, lax.div(turn, 2)) + differ(self.x, lax.rem(turn, 2))

    def over_seq(self, turn):
        return {"seq": self.shard(turn)}

    def over_core(self):
        return {"grp": 2 * self.z + 1 - self.c}

    def z_of(self, step):
        return lax.rem(self.z + step, self.depth)

    def over_grp(self, step):
        return {"grp": lax.rem(self.grp + step, 2 * self.depth)}

    def over_z(self, step):
        return {"grp": 2 * self.z_of(step) + self.c}

    def step_of(self, axis, step):
        if axis == "s":
            return self.shard(step)
        return self.z_of(step) if axis == "z" else 1 - self.own[axis]

    def others(self, axis):
        if axis == "z":
            return [self.over_z(step) for step in range(1, self.depth)]
        if axis == "s":
            return [self.over_seq(turn) for turn in (1, 2, 3)]
        return [self.over_seq({"x": 1, "y": 2}[axis])]

    def greet(self, beyond=True):
        peers = [self.over_seq(turn) for turn in (1, 2, 3)]
        if beyond:
            peers += [self.over_grp(step) for step in range(1, 2 * self.depth)]
        barrier = pltpu.get_barrier_semaphore()
        for peer in peers:
            pl.semaphore_signal(barrier, inc=1, device_id=peer, device_id_type=MESH)
        pl.semaphore_wait(barrier, len(peers))


def copy_to(source, target, sems, index, peer):
    send, recv = sems
    return pltpu.make_async_remote_copy(
        src_ref=source,
        dst_ref=target,
        send_sem=send.at[index],
        recv_sem=recv.at[index],
        device_id=peer,
        device_id_type=MESH,
    )


class Gather:
    def __init__(self, place, view, sems, base, order, own=None):
        self.at, self.view, self.sems, self.base, self.order = place, view, sems, base, order
        self.own = own

    def moves(self, stage):
        p = self.at
        done = self.order[:stage]
        where = [pl.ds(0, p.size[axis]) if axis in done else p.own[axis] for axis in "yxz"]
        region = self.view(*where, p.c)
        if stage == 3:
            return [(region, p.depth + 1, p.over_core())]
        base = sum(p.size[axis] - 1 for axis in done)
        return [(region, base + i, peer) for i, peer in enumerate(p.others(self.order[stage]))]

    def copies(self, stage):
        source = self.own if stage == 0 else None
        return [
            copy_to(r if source is None else source, r, self.sems, self.base + slot, peer)
            for r, slot, peer in self.moves(stage)
        ]

    def place_own(self, sem):
        p = self.at
        return pltpu.make_async_copy(self.own, self.view(p.y, p.x, p.z, p.c), sem)

    def step(self, stage):
        if stage:
            for made in self.copies(stage - 1):
                made.wait()
        if stage < 4:
            for made in self.copies(stage):
                made.start()


def gather_slots(depth):
    return depth + 2


def bind(ref, first, count):
    return lambda *i: ref.at[(pl.ds(first, count),) + i]


def bind_rows(ref, first, count):
    return lambda *i: ref.at[i + (pl.ds(first, count),)]


class Scatter:
    def __init__(self, place, view, out, bufs, sems, base, order, far=None):
        self.far = far or view
        self.at, self.view, self.out, self.sems, self.base, self.order = place, view, out, sems, base, order
        self.get_core, self.give, self.get, self.keep = bufs

    def plan(self, number):
        p = self.at
        axis = self.order[number]
        rest = [other for other in sorted(self.order) if other not in self.order[: number + 1]]
        combos = [{}]
        for other in rest:
            combos = [{**c, other: i} for c in combos for i in range(p.size[other])]
        first = 0
        for k in range(number):
            left = 1
            for other in self.order[k + 1 :]:
                left *= p.size[other]
            first += left * (p.size[self.order[k]] - 1)
        return axis, combos, first

    def kept(self, index):
        p = self.at
        linear = 0
        for axis in sorted(self.order):
            if axis != self.order[0]:
                linear = linear * p.size[axis] + index.get(axis, p.own[axis])
        return linear

    def now(self, number, index):
        p = self.at
        if number:
            return self.keep[self.kept(index)]
        where = {axis: index.get(axis, p.own[axis]) for axis in self.order}
        if "s" in where:
            where["y"], where["x"] = lax.div(where["s"], 2), lax.rem(where["s"], 2)
        where = [where[axis] for axis in "yxz"]
        lead = (slice(None),) * (len(self.get_core.shape) - 5)
        return self.view(*where, p.c)[...].astype(WIDE) + self.get_core[lead + tuple(where)].astype(WIDE)

    def copies(self, stage):
        p = self.at
        if stage == 0:
            source = self.far(pl.ds(0, 2), pl.ds(0, 2), pl.ds(0, p.depth), 1 - p.c)
            return [copy_to(source, self.get_core, self.sems, self.base, p.over_core())]
        axis, combos, first = self.plan(stage - 1)
        slot = 1 + sum(p.size[other] - 1 for other in self.order[: stage - 1])
        made = []
        for i, peer in enumerate(p.others(axis)):
            here = pl.ds(first + i * len(combos), len(combos))
            made.append(copy_to(self.give.at[here], self.get.at[here], self.sems, self.base + slot + i, peer))
        return made

    def step(self, stage):
        p = self.at
        last = len(self.order) + 1
        if stage:
            for made in self.copies(stage - 1):
                made.wait()
        if stage >= 2:
            axis, combos, first = self.plan(stage - 2)
            for k, index in enumerate(combos):
                total = self.keep[self.kept(index)]
                for i in range(p.size[axis] - 1):
                    total = total + self.get[first + i * len(combos) + k].astype(WIDE)
                if stage == last:
                    self.out(total)
                else:
                    self.keep[self.kept(index)] = total
        if 1 <= stage < last:
            axis, combos, first = self.plan(stage - 1)
            for i in range(p.size[axis] - 1):
                for k, index in enumerate(combos):
                    target = {**index, axis: p.step_of(axis, i + 1)}
                    self.give[first + i * len(combos) + k] = self.now(stage - 1, target).astype(LOW)
        if stage < last:
            for made in self.copies(stage):
                made.start()
        if stage == 1:
            axis, combos, first = self.plan(0)
            for index in combos:
                self.keep[self.kept(index)] = self.now(0, index)


def scatter_slots(depth):
    return depth + 3


def scatter_scratch(depth, order, shape):
    kept = {"z": 4, "s": depth}.get(order[0], 2 * depth)
    return [
        pltpu.VMEM(shape[:-2] + (2, 2, depth) + shape[-2:], LOW),
        pltpu.VMEM((4 * depth - 1,) + shape, LOW),
        pltpu.VMEM((4 * depth - 1,) + shape, LOW),
        pltpu.VMEM((kept,) + shape, WIDE),
    ]


class SumTile:
    def __init__(self, place, out, give, get, sems, base):
        self.at, self.out, self.give, self.get, self.sems, self.base = place, out, give, get, sems, base

    def copies(self, stage):
        p = self.at
        if stage == 0:
            moves = [(p.shard(turn), turn - 1, p.over_seq(turn)) for turn in (1, 2, 3)]
        else:
            moves = [(4, 2 + step, p.over_grp(step)) for step in range(1, 2 * p.depth)]
        return [
            copy_to(self.give.at[a], self.get.at[b], self.sems, self.base + b, peer) for a, b, peer in moves
        ]

    def step(self, stage):
        if stage:
            for made in self.copies(stage - 1):
                made.wait()
        if stage == 1:
            self.give[4] = (self.give[self.at.seq] + self.get[0]) + (self.get[1] + self.get[2])
        if stage == 2:
            total = self.give[4]
            for step in range(1, 2 * self.at.depth):
                total = total + self.get[2 + step]
            self.out[...] = total
            return
        for made in self.copies(stage):
            made.start()


def run(steps):
    for piece, stage in steps:
        piece.step(stage)


def skewed(pieces, stages):
    stages = list(stages)
    return [
        (piece, stages[slot - k])
        for slot in range(len(pieces) + len(stages) - 1)
        for k, piece in enumerate(pieces)
        if 0 <= slot - k < len(stages)
    ]


def unit_rows_of(values):
    centred = values - jnp.mean(values, axis=-1, keepdims=True)
    factor = lax.rsqrt(jnp.mean(centred * centred, axis=-1, keepdims=True) + NORM_EPSILON)
    return centred * factor, factor


def put_tiles(ref, here, value):
    for k in range(ref.shape[0]):
        ref[k, here, :] = value[:, 128 * k : 128 * (k + 1)]


def get_tiles(ref, here):
    return jnp.concatenate([ref[k, here, :] for k in range(ref.shape[0])], axis=1)


def hide_future(scores, first_slot, first_row):
    slot = lax.broadcasted_iota(jnp.int32, scores.shape, 0) + first_slot
    row = lax.broadcasted_iota(jnp.int32, scores.shape, 1) + first_row
    return jnp.where(3 * slot <= row, scores, MASKED_SCORE)


def span(number, size):
    return pl.ds(pl.multiple_of(number * size, size), size)


def front_kernel(depth, tok, wq, wm, wo, wu, wd, vec, *refs):
    early_out, late, down, vectors, edge, qh_out, kv_out, mixed_out, lse, attended = refs[:10]
    tiles, wide_a, low_a, qs, ms, kvt, own_late, own_down, tile, early, qh, kv, mixed = refs[10:23]
    gsend, grecv, xsend, xrecv, lsem, osem = refs[23:]
    p = Place(depth)
    own = (p.y, p.x, p.z, p.c)
    rows, width = tok.shape
    slots = rows // 3
    size = qh.shape[1]
    lanes = 2 * size
    shard_lanes = vec.shape[1]
    tile[...] = jnp.zeros_like(tile)
    tile[0 : vec.shape[0], 0:shard_lanes] = vec[...]
    tiles[own] = pltpu.roll(tile[...], p.grp * shard_lanes, 1).astype(LOW)
    early[(0,) + own] = wq[...].astype(LOW)
    for tap in range(3):
        for half in range(2):
            columns = []
            for head in range(4 * half, 4 * half + 4):
                columns.append(wm[tap, :, head * size : (head + 1) * size])
                columns.append(wm[tap, :, width + head * size : width + (head + 1) * size])
            early[(1 + 3 * half + tap,) + own] = jnp.concatenate(columns, axis=1).astype(LOW)
    own_late[0] = wo[...].astype(LOW)
    for part in range(4):
        own_late[1 + part] = wu[:, part * width : (part + 1) * width].astype(LOW)
    own_down[...] = wd[...].astype(LOW)
    p.greet()
    half_down = down.shape[4] // 2
    views = [
        (lambda *i: tiles.at[i], "zxy", None),
        (bind(early, 0, 1), "zxy", None),
        (bind(early, 1, 1), "zyx", None),
        (bind(early, 2, 1), "zxy", None),
        (bind(early, 3, 1), "yzx", None),
        (bind(early, 4, 1), "zyx", None),
        (bind(early, 5, 1), "xzy", None),
        (bind(early, 6, 1), "xyz", None),
        (bind(late, 0, 3), "xyz", own_late.at[pl.ds(0, 3)]),
        (bind(late, 3, 2), "yzx", own_late.at[pl.ds(3, 2)]),
        (bind_rows(down, 0, half_down), "xzy", own_down.at[pl.ds(0, half_down)]),
        (bind_rows(down, half_down, half_down), "yxz", own_down.at[pl.ds(half_down, half_down)]),
    ]
    step = gather_slots(depth)
    pieces = [
        Gather(p, view, (gsend, grecv), step * k, order, first) for k, (view, order, first) in enumerate(views)
    ]
    vector_piece, query_piece, soon, later = pieces[0], pieces[1], pieces[2:8], pieces[8:]
    for piece in pieces[:8]:
        piece.step(0)
    for k, piece in enumerate(later):
        piece.place_own(lsem.at[k]).start()
        piece.step(0)

    block = 128

    @pl.loop(0, rows // block)
    def _(number):
        at = pl.multiple_of(number * block, block)
        unit, _ = unit_rows_of(tok[pl.ds(at, block), :].astype(WIDE))
        put_tiles(wide_a, pl.ds(at + 8, block), unit)

    for stage in (1, 2):
        vector_piece.step(stage)
        query_piece.step(stage)
    for piece in soon[2:3] + soon[4:] + soon[:2] + soon[3:4]:
        piece.step(1)
    vector_piece.step(3)
    query_piece.step(3)
    vector_piece.step(4)
    tile_lanes = tiles.shape[-1]
    for y in range(2):
        for x in range(2):
            total = jnp.zeros(tiles.shape[-2:], WIDE)
            for z in range(depth):
                for c in range(2):
                    total += tiles[y, x, z, c].astype(WIDE)
            s = 2 * y + x
            vectors[:, s * tile_lanes : (s + 1) * tile_lanes] = total
    gain, shift = vectors[0:1, :], vectors[1:2, :]

    @pl.loop(0, rows // block)
    def _(number):
        at = pl.multiple_of(number * block, block)
        normed = (get_tiles(wide_a, pl.ds(at + 8, block)) * gain + shift).astype(LOW)
        low_a[pl.ds(at, block), :] = normed
        put_tiles(wide_a, pl.ds(at + 8, block), normed.astype(WIDE))

    def query_copy(half, turn):
        return copy_to(
            qs.at[half, p.shard(turn)],
            qh.at[half, :, span(p.seq, rows)],
            (xsend, xrecv),
            7 + 3 * half + turn - 1,
            p.over_seq(turn),
        )

    def send_queries(half):
        for turn in (1, 2, 3):
            query_copy(half, turn).start()
        qh[half, :, span(p.seq, rows)] = qs[half, p.seq]

    last = p.seq == 3

    def edge_copy():
        return copy_to(
            wide_a.at[:, pl.ds(rows, 8)], wide_a.at[:, pl.ds(0, 8)], (xsend, xrecv), 0, {"seq": lax.rem(p.seq + 1, 4)}
        )

    @pl.when(jnp.logical_not(last))
    def _():
        edge_copy().start()

    query_piece.step(4)
    turned = lax.dot_general(early[0].reshape(width, width).T, low_a[...], NT, preferred_element_type=WIDE)
    qs[...] = turned.astype(LOW).reshape(qs.shape)
    for piece in soon[5:] + soon[:2] + soon[3:4] + soon[2:3] + soon[4:5]:
        piece.step(2)
    send_queries(0)
    for k, piece in enumerate(later):
        piece.place_own(lsem.at[k]).wait()
        piece.step(1)
    for piece in soon:
        piece.step(3)
    for piece in later[:1] + later[3:]:
        piece.step(2)
    for piece in soon:
        piece.step(4)

    @pl.when(p.seq > 0)
    def _():
        edge_copy().wait_recv()

    @pl.when(jnp.logical_not(last))
    def _():
        edge_copy().wait_send()

    @pl.when(p.seq == 0)
    def _():
        wide_a[:, 0:8, :] = jnp.zeros((width // 128, 8, 128), WIDE)

    edge[...] = wide_a[:, 0:8, :]
    parts = rows // PART
    strips = qh.shape[2] // STRIP

    def early_leaves():
        return pltpu.make_async_copy(early, early_out, osem.at[0])

    def kv_leaves(half):
        return pltpu.make_async_copy(kv.at[half], kv_out.at[half], osem.at[1 + half])

    def qh_leaves(half):
        return pltpu.make_async_copy(qh.at[half], qh_out.at[half], osem.at[3 + half])

    def mixed_leaves(half, strip, index):
        here = span(strip, STRIP)
        return pltpu.make_async_copy(mixed.at[half, :, here], mixed_out.at[half, :, here], osem.at[index])

    def mixed_stays(half, part):
        return pltpu.make_async_copy(
            mixed.at[half, :, span(p.seq * parts + part, PART)],
            attended.at[half, p.seq, :, span(part, PART)],
            osem.at[5 + 2 * strips + half * parts + part],
        )

    early_leaves().start()

    def weight(j):
        return early[j].reshape(width, width)

    mine = span(p.seq, slots)

    def memory_copy(half, turn):
        return copy_to(
            ms.at[half, :, span(p.shard(turn), lanes)],
            kv.at[half, mine],
            (xsend, xrecv),
            1 + 3 * half + turn - 1,
            p.over_seq(turn),
        )

    def project(half):
        for tap in range(3):
            window = get_tiles(wide_a, pl.ds(6 + tap, slots, stride=3)).astype(LOW)
            part = dot(window, weight(1 + 3 * half + tap))
            total = part if tap == 0 else total + part
        ms[half] = total.astype(LOW)
        for turn in (3, 1, 2):
            memory_copy(half, turn).start()
        kv[half, mine, :] = ms[half, :, span(p.seq, lanes)]

    project(0)
    project(1)
    send_queries(1)
    for turn in (1, 2, 3):
        memory_copy(0, turn).wait()
    kvt[0] = kv[0].T
    kv_leaves(0).start()

    def mixed_copy(half, turn, part):
        shard = p.shard(turn)
        return copy_to(
            mixed.at[half, :, span(shard * parts + part, PART)],
            attended.at[half, p.seq, :, span(part, PART)],
            (xsend, xrecv),
            13 + (3 * half + turn - 1) * parts + part,
            p.over_seq(turn),
        )

    def attend(half, seen, strip):
        here = span(strip, STRIP)
        queries = qh[half, :, here] * jnp.bfloat16(size ** (-0.5))
        queries = jnp.concatenate([queries, jnp.zeros_like(queries)], axis=0)
        whole = seen - SLOTS
        scores = hide_future(dot(kv[half, whole:seen, :], queries), whole, strip * STRIP)
        if whole:
            scores = jnp.concatenate([dot(kv[half, 0:whole, :], queries), scores], axis=0)
        highest = jnp.max(scores, axis=0, keepdims=True)
        exponent = jnp.exp(scores - highest)
        summed = jnp.sum(exponent, axis=0, keepdims=True)
        out = dot(kvt[half, size:lanes, 0:seen], exponent.astype(LOW)) * (1.0 / summed)
        lse[half, strip] = highest + jnp.log(summed)
        mixed[half, :, here] = out.astype(LOW)

    def work(half):
        @pl.loop(0, strips)
        def _(it):
            for number, turn in ((1, 1), (3, 2), (4, 3)):

                @pl.when(it == number)
                def _():
                    query_copy(half, turn).wait()

            strip = p.strip(it)
            for group in range(strips):

                @pl.when(strip == group)
                def _():
                    attend(half, SLOTS * (group + 1), strip)

            mixed_leaves(half, strip, 5 + half * strips + it).start()
            for k in range(2):
                granule = 2 * strip + k
                shard, part = lax.div(granule, parts), lax.rem(granule, parts)
                turn = p.turn_to(shard)

                @pl.when(turn > 0)
                def _():
                    mixed_copy(half, turn, part).start()

                @pl.when(turn == 0)
                def _():
                    mixed_stays(half, part).start()

            @pl.when(it == (5, 3)[half])
            def _():
                for piece in later[1:3]:
                    piece.step(2 + half)

    work(0)
    for turn in (1, 2, 3):
        memory_copy(1, turn).wait()
    kvt[1] = kv[1].T
    kv_leaves(1).start()
    qh_leaves(0).start()
    work(1)
    qh_leaves(1).start()
    for piece in later[:1] + later[3:]:
        piece.step(3)
    for piece in later:
        piece.step(4)
    early_leaves().wait()
    for half in range(2):
        kv_leaves(half).wait()
        qh_leaves(half).wait()
        for it in range(strips):
            mixed_leaves(half, p.strip(it), 5 + half * strips + it).wait()
        for part in range(parts):
            mixed_stays(half, part).wait()
            for turn in (1, 2, 3):
                mixed_copy(half, turn, part).wait()


def front(tok, params):
    wq, wm, wo, wu, wd, vec = params
    groups = lax.axis_size("grp")
    depth = groups // 2
    rows, width = tok.shape
    own, slots, size = wq.shape[0], rows // 3, width // H
    lanes = 2 * size
    tile_lanes = vec.shape[1] * groups
    whole = (2, 2, depth, 2)
    sems = pltpu.SemaphoreType.DMA((12 * gather_slots(depth),))
    parts = rows // PART
    swaps = pltpu.SemaphoreType.DMA((13 + 6 * parts,))
    anywhere = pl.BlockSpec(memory_space=pl.ANY)
    vmem = pl.BlockSpec(memory_space=pltpu.VMEM)
    return pl.pallas_call(
        functools.partial(front_kernel, depth),
        out_shape=(
            shaped(EARLY, *whole, own, width),
            shaped(LATE, *whole, own, width),
            shaped(*whole, *wd.shape),
            shaped(ROWS, 4 * tile_lanes, kind=WIDE),
            shaped(width // 128, 8, 128, kind=WIDE),
            shaped(2, size, 4 * rows),
            shaped(2, 4 * slots, lanes),
            shaped(2, size, 4 * rows),
            shaped(2, 4 * rows // STRIP, 1, STRIP, kind=WIDE),
            shaped(2, 4, size, rows),
        ),
        in_specs=in_vmem(7),
        out_specs=[anywhere] * 3 + [vmem] * 2 + [anywhere] * 3 + [vmem, anywhere],
        scratch_shapes=[
            pltpu.VMEM((*whole, ROWS, tile_lanes), LOW),
            pltpu.VMEM((width // 128, rows + 8, 128), WIDE),
            pltpu.VMEM((rows, width), LOW),
            pltpu.VMEM((2, 4, size, rows), LOW),
            pltpu.VMEM((2, slots, width), LOW),
            pltpu.VMEM((2, lanes, 4 * slots), LOW),
            pltpu.VMEM((LATE, own, width), LOW),
            pltpu.VMEM(wd.shape, LOW),
            pltpu.VMEM((ROWS, tile_lanes), WIDE),
            pltpu.VMEM((EARLY, *whole, own, width), LOW),
            pltpu.VMEM((2, size, 4 * rows), LOW),
            pltpu.VMEM((2, 4 * slots, lanes), LOW),
            pltpu.VMEM((2, size, 4 * rows), LOW),
            sems,
            sems,
            swaps,
            swaps,
            pltpu.SemaphoreType.DMA((4,)),
            pltpu.SemaphoreType.DMA((5 + 2 * (4 * rows // STRIP) + 2 * parts,)),
        ],
        compiler_params=pltpu.CompilerParams(
            collective_id=0, has_side_effects=True, vmem_limit_bytes=58 * MEGA
        ),
    )(tok, wq, wm, wo, wu, wd, vec)


def middle_kernel(depth, tok_in, cot_in, att_in, late_in, down_in, vec, length, *refs):
    out_to, dres_to, doh, g_stack_to, g_down_to, g_vec = refs[:6]
    tok, cot, att, late, down, out, dres, g_stack, g_down = refs[6:15]
    zs, dus, cs, es, ys, dos, xsend, xrecv, isem, osem, gsem = refs[15:]
    p = Place(depth)
    arriving = [
        pltpu.make_async_copy(source, target, isem.at[k])
        for k, (source, target) in enumerate(
            ((att_in, att), (tok_in, tok), (late_in, late), (down_in, down), (cot_in, cot))
        )
    ]
    for made in arriving:
        made.start()
    p.greet(beyond=False)
    rows, width = tok.shape
    hidden = zs.shape[1]
    gain, shift, bias = vec[2:3, :], vec[3:4, :], vec[4:5, :]
    inner = 0.7978845608028654
    cubic = inner * 0.044715
    g_vec[...] = jnp.zeros_like(g_vec)

    parts = rows // PART

    def do_copy(number, turn):
        return copy_to(
            dos.at[:, p.shard(turn), :, span(number, PART)],
            doh.at[:, :, span(p.seq * parts + number, PART)],
            (xsend, xrecv),
            3 * number + turn - 1,
            p.over_seq(turn),
        )

    def leave(number):
        here = span(number, PART)
        pairs = (
            (out.at[here], out_to.at[here]),
            (dres.at[here], dres_to.at[here]),
            (dos.at[:, p.seq, :, here], doh.at[:, :, span(p.seq * parts + number, PART)]),
        )
        return [pltpu.make_async_copy(a, b, osem.at[3 * number + k]) for k, (a, b) in enumerate(pairs)]

    for made in arriving:
        made.wait()

    @pl.loop(0, parts)
    def _(number):
        at = pl.multiple_of(number * PART, PART)
        here = pl.ds(at, PART)
        attended = att[:, :, :, here].reshape(width, PART).T
        residual = tok[here, :].astype(WIDE) + dot(attended, late[0])
        unit, factor = unit_rows_of(residual)
        normed = (unit * gain + shift).astype(LOW)
        cs[here, :] = normed
        place = lax.broadcasted_iota(jnp.int32, (PART, 1), 0) + (p.seq * rows + at)
        live = (place < length[0, 0]).astype(WIDE)
        upstream = cot[here, :].astype(WIDE) * live
        upstream_low = upstream.astype(LOW)
        es[here, :] = upstream_low
        result = residual + bias
        back = jnp.zeros((PART, width), WIDE)
        for part in range(hidden // width):
            here_hidden = pl.ds(part * width, width)
            u = dot(normed, late[1 + part]) + vec[5 + part : 6 + part, :]
            square = u * u
            half = 0.5 + 0.5 * jnp.tanh(u * (inner + cubic * square))
            active = u * half
            slope = half + active * (1.0 - half) * (2.0 * inner + 6.0 * cubic * square)
            active_low = active.astype(LOW)
            zs[here, here_hidden] = active_low
            result += dot(active_low, down[here_hidden, :])
            pulled = lax.dot_general(upstream_low, down[here_hidden, :], NT, preferred_element_type=WIDE)
            grad = (pulled * slope).astype(LOW)
            dus[here, here_hidden] = grad
            g_vec[5 + part : 6 + part, :] += jnp.sum(grad.astype(WIDE), axis=0, keepdims=True)
            back += lax.dot_general(grad, late[1 + part], NT, preferred_element_type=WIDE)
        out[here, :] = result.astype(LOW)
        scaled = back * gain
        total = upstream + factor * (
            scaled
            - jnp.mean(scaled, axis=-1, keepdims=True)
            - unit * jnp.mean(scaled * unit, axis=-1, keepdims=True)
        )
        dres[here, :] = total
        branch = total.astype(LOW)
        ys[here, :] = branch
        turned = lax.dot_general(late[0], branch, NT, preferred_element_type=WIDE)
        dos[:, :, :, here] = turned.astype(LOW).reshape(dos.shape[:3] + (PART,))
        for turn in (3, 1, 2):
            do_copy(number, turn).start()
        for made in leave(number):
            made.start()
        g_vec[2:3, :] += jnp.sum(back * unit, axis=0, keepdims=True)
        g_vec[3:4, :] += jnp.sum(back, axis=0, keepdims=True)
        g_vec[4:5, :] += jnp.sum(upstream, axis=0, keepdims=True)

    def finished(ref, target, index):
        made = pltpu.make_async_copy(ref, target, gsem.at[index])
        made.start()
        return made

    left = []
    for part in range(hidden // width):
        piece = pl.ds(part * width, width)
        g_down[piece, :] = over_rows(zs[:, piece], es[...]).astype(LOW)
        left.append(finished(g_down.at[piece], g_down_to.at[piece], 5 + part))
    g_stack[0] = dot(att[...].reshape(width, rows), ys[...]).astype(LOW)
    left.append(finished(g_stack.at[0], g_stack_to.at[0], 0))
    for part in range(hidden // width):
        piece = pl.ds(part * width, width)
        g_stack[1 + part] = over_rows(cs[...], dus[:, piece]).astype(LOW)
        left.append(finished(g_stack.at[1 + part], g_stack_to.at[1 + part], 1 + part))
    for number in range(parts):
        for turn in (1, 2, 3):
            do_copy(number, turn).wait()
        for made in leave(number):
            made.wait()
    for made in left:
        made.wait()


def middle(tok, cot, att, late, down, vec, length):
    rows, width = tok.shape
    hidden = down.shape[0]
    sems = pltpu.SemaphoreType.DMA((3 * (rows // PART),))
    return pl.pallas_call(
        functools.partial(middle_kernel, lax.axis_size("grp") // 2),
        out_shape=(
            shaped(rows, width),
            shaped(rows, width, kind=WIDE),
            shaped(2, width // H, 4 * rows),
            shaped(LATE, width, width),
            shaped(hidden, width),
            shaped(*vec.shape, kind=WIDE),
        ),
        in_specs=[pl.BlockSpec(memory_space=pl.ANY)] * 5
        + [pl.BlockSpec(memory_space=pltpu.VMEM), pl.BlockSpec(memory_space=pltpu.SMEM)],
        out_specs=[pl.BlockSpec(memory_space=pl.ANY)] * 5 + [pl.BlockSpec(memory_space=pltpu.VMEM)],
        scratch_shapes=[pltpu.VMEM(x.shape, x.dtype) for x in (tok, cot, att, late, down)]
        + [
            pltpu.VMEM((rows, width), LOW),
            pltpu.VMEM((rows, width), WIDE),
            pltpu.VMEM((LATE, width, width), LOW),
            pltpu.VMEM((hidden, width), LOW),
            pltpu.VMEM((rows, hidden), LOW),
            pltpu.VMEM((rows, hidden), LOW),
            pltpu.VMEM((rows, width), LOW),
            pltpu.VMEM((rows, width), LOW),
            pltpu.VMEM((rows, width), LOW),
            pltpu.VMEM(att.shape, LOW),
            sems,
            sems,
            pltpu.SemaphoreType.DMA((5,)),
            sems,
            pltpu.SemaphoreType.DMA((LATE + hidden // width,)),
        ],
        compiler_params=pltpu.CompilerParams(
            collective_id=1, has_side_effects=True, vmem_limit_bytes=58 * MEGA
        ),
    )(tok, cot, att, late, down, vec, length)


def back_kernel(depth, *refs):
    far_inputs, (lse, vec, edge, g_vec) = refs[:9], refs[9:13]
    grad, out_early, out_late, out_down, out_vec = refs[13:18]
    scatter, refs = refs[18:54], refs[54:]
    near_inputs, refs = refs[:9], refs[9:]
    tok, kv, doh, qh, mixed, g_late, g_down, early, dres = near_inputs
    g_early, dkv, kvt, dqs, dq, dms, dm, wide_a, low_a, wide_da, da, after, give, get, out_sum = refs[:15]
    rsend, rrecv, xsend, xrecv, isem = refs[15:]
    p = Place(depth)
    arriving = [
        pltpu.make_async_copy(a, b, isem.at[k]) for k, (a, b) in enumerate(zip(far_inputs, near_inputs))
    ]
    for made in arriving:
        made.start()
    rows, width = tok.shape
    slots = rows // 3
    size = qh.shape[1]
    lanes = 2 * size
    scale = size ** (-0.5)
    parts = rows // PART
    strips = qh.shape[2] // STRIP
    step = scatter_slots(depth)
    p.greet()

    def out_to(ref, first, count):
        def put(value):
            ref[first : first + count] = value

        return put

    half_down = g_down.shape[4] // 2
    todo = [
        (bind(g_late, 0, 3), out_to(out_late, 0, 3), bind(far_inputs[5], 0, 3)),
        (bind(g_late, 3, 2), out_to(out_late, 3, 2), bind(far_inputs[5], 3, 2)),
        (bind_rows(g_down, 0, half_down), out_to(out_down, 0, half_down), bind_rows(far_inputs[6], 0, half_down)),
        (
            bind_rows(g_down, half_down, half_down),
            out_to(out_down, half_down, half_down),
            bind_rows(far_inputs[6], half_down, half_down),
        ),
        (bind(g_early, 0, 1), out_to(out_early, 0, 1), None),
        (bind(g_early, 1, 2), out_to(out_early, 1, 2), None),
        (bind(g_early, 3, 1), out_to(out_early, 3, 1), None),
        (bind(g_early, 4, 2), out_to(out_early, 4, 2), None),
        (bind(g_early, 6, 1), out_to(out_early, 6, 1), None),
    ]
    pieces = [
        Scatter(p, view, out, scatter[4 * k : 4 * k + 4], (rsend, rrecv), step * k, SCATTER_ORDERS[k], far)
        for k, (view, out, far) in enumerate(todo)
    ]
    soon, query, first, second = pieces[:4], pieces[4:5], pieces[5:7], pieces[7:]
    small = SumTile(p, out_vec, give, get, (rsend, rrecv), step * len(pieces))
    for piece in soon:
        piece.step(0)
    gain, shift = vec[0:1, :], vec[1:2, :]
    block = 128
    wide_a[:, 0:8, :] = edge[...]
    arriving[0].wait()

    @pl.loop(0, rows // block)
    def _(number):
        at = pl.multiple_of(number * block, block)
        unit, _ = unit_rows_of(tok[pl.ds(at, block), :].astype(WIDE))
        normed = (unit * gain + shift).astype(LOW)
        low_a[pl.ds(at, block), :] = normed
        put_tiles(wide_a, pl.ds(at + 8, block), normed.astype(WIDE))

    for made in arriving[1:5]:
        made.wait()
    for half in range(2):
        kvt[half] = kv[half].T
    dkv[...] = jnp.zeros_like(dkv)

    def dq_copy(half, turn, part):
        return copy_to(
            dqs.at[half, :, span(p.shard(turn) * parts + part, PART)],
            dq.at[half, p.seq, :, span(part, PART)],
            (xsend, xrecv),
            (3 * half + turn - 1) * parts + part,
            p.over_seq(turn),
        )

    def attend(half, seen, strip):
        here = span(strip, STRIP)
        queries = qh[half, :, here] * jnp.bfloat16(scale)
        incoming = doh[half, :, here]
        middle = jnp.sum(incoming.astype(WIDE) * mixed[half, :, here].astype(WIDE), axis=0, keepdims=True)
        blank = jnp.zeros_like(queries)
        queries = jnp.concatenate([queries, blank], axis=0)
        incoming = jnp.concatenate([blank, incoming], axis=0)
        total = lse[half, strip]
        turned = jnp.zeros((size, STRIP), WIDE)
        for start in range(0, seen, 2 * SLOTS):
            stop = min(start + 2 * SLOTS, seen)
            keys = kv[half, start:stop, :]
            scores = dot(keys, queries)
            if stop == seen:
                clear = stop - SLOTS - start
                masked = hide_future(scores[clear:], stop - SLOTS, strip * STRIP)
                scores = jnp.concatenate([scores[:clear], masked], axis=0) if clear else masked
            weights = jnp.exp(scores - total)
            slope = (weights * (dot(keys, incoming) - middle)).astype(LOW)
            dkv[half, start:stop, :] += lax.dot_general(
                slope, queries, NT, preferred_element_type=WIDE
            ) + lax.dot_general(weights.astype(LOW), incoming, NT, preferred_element_type=WIDE)
            turned += dot(kvt[half, 0:size, start:stop], slope)
        dqs[half, :, here] = (turned * scale).astype(LOW)

    def memory_copy(half, turn):
        return copy_to(
            dms.at[half, span(p.shard(turn), slots)],
            dm.at[half, :, span(p.seq, lanes)],
            (xsend, xrecv),
            6 * parts + 3 * half + turn - 1,
            p.over_seq(turn),
        )

    def send_memory(half):
        dms[half] = dkv[half].astype(LOW)
        for turn in (3, 1, 2):
            memory_copy(half, turn).start()
        dm[half, :, span(p.seq, lanes)] = dms[half, span(p.seq, slots), :]

    def put_early(j, value):
        g_early[j] = value.astype(LOW).reshape(g_early.shape[1:])

    def memory_gradient(half, tap):
        window = get_tiles(wide_a, pl.ds(6 + tap, slots, stride=3)).astype(LOW)
        put_early(1 + 3 * half + tap, over_rows(window, dm[half]))

    @pl.loop(0, 2 * strips)
    def _(turn_number):
        half, it = lax.div(turn_number, strips), lax.rem(turn_number, strips)

        @pl.when(turn_number == strips)
        def _():
            send_memory(0)

        @pl.when(turn_number == strips + 2)
        def _():
            for turn in (1, 2, 3):
                memory_copy(0, turn).wait()
            for tap in range(3):
                memory_gradient(0, tap)
            for piece in first:
                piece.step(0)

        strip = p.strip(strips - 1 - it)
        for group in range(strips):

            @pl.when(strip == group)
            def _():
                attend(half, SLOTS * (group + 1), strip)

        for k in range(2):
            granule = 2 * strip + k
            shard, part = lax.div(granule, parts), lax.rem(granule, parts)
            turn = p.turn_to(shard)

            @pl.when(turn > 0)
            def _():
                dq_copy(half, turn, part).start()

            @pl.when(turn == 0)
            def _():
                dq[half, p.seq, :, span(part, PART)] = dqs[half, :, span(granule, PART)]

        @pl.when(turn_number == 1)
        def _():
            for k in (5, 6):
                pltpu.make_async_copy(far_inputs[k], near_inputs[k], isem.at[k]).wait()

        for when, steps in (
            (1, [(piece, 1) for piece in soon]),
            (7, [(piece, 2) for piece in soon]),
            (9, [(piece, 1) for piece in first]),
            (10, [(piece, 3) for piece in soon]),
        ):

            @pl.when(turn_number == when)
            def _():
                run(steps)

    send_memory(1)
    for half in range(2):
        for turn in (1, 2, 3):
            for part in range(parts):
                dq_copy(half, turn, part).wait()
    for made in arriving[7:]:
        made.wait()
    turned = dq[...].reshape(width, rows)
    put_early(0, dot(turned, low_a[...]).T)
    query[0].step(0)
    da[...] = lax.dot_general(turned.T, early[0], NT, preferred_element_type=WIDE)
    query[0].step(1)
    run([(piece, 2) for piece in first])
    for turn in (1, 2, 3):
        memory_copy(1, turn).wait()
    for tap in range(3):
        memory_gradient(1, tap)
        if tap:
            second[tap - 1].step(0)
    wide_da[:, 0:8, :] = jnp.zeros((width // 128, 8, 128), WIDE)
    for tap in range(3):
        pulled = lax.dot_general(dm[0], early[1 + tap], NT, preferred_element_type=WIDE)
        pulled += lax.dot_general(dm[1], early[4 + tap], NT, preferred_element_type=WIDE)
        put_tiles(wide_da, pl.ds(6 + tap, slots, stride=3), pulled)

    def edge_copy():
        return copy_to(
            wide_da.at[:, pl.ds(0, 8)], after, (xsend, xrecv), 6 * parts + 6, {"seq": lax.rem(p.seq + 3, 4)}
        )

    @pl.when(p.seq > 0)
    def _():
        edge_copy().start()

    run([(piece, 1) for piece in second])
    run([(piece, 4) for piece in soon])
    run([(query[0], 2), (first[0], 3), (first[1], 3)])

    @pl.when(p.seq < 3)
    def _():
        edge_copy().wait_recv()

    @pl.when(p.seq > 0)
    def _():
        edge_copy().wait_send()

    @pl.when(p.seq == 3)
    def _():
        after[...] = jnp.zeros_like(after)

    wide_da[:, rows + 6 : rows + 8, :] = after[:, 6:8, :]
    out_sum[...] = g_vec[...]

    @pl.loop(0, rows // block)
    def _(number):
        at = pl.multiple_of(number * block, block)
        here = pl.ds(at, block)
        unit, factor = unit_rows_of(tok[here, :].astype(WIDE))
        upstream = da[here, :] + get_tiles(wide_da, pl.ds(at + 8, block))
        scaled = upstream * gain
        inward = factor * (
            scaled
            - jnp.mean(scaled, axis=-1, keepdims=True)
            - unit * jnp.mean(scaled * unit, axis=-1, keepdims=True)
        )
        grad[here, :] = (dres[here, :] + inward).astype(LOW)
        out_sum[0:1, :] += jnp.sum(upstream * unit, axis=0, keepdims=True)
        out_sum[1:2, :] += jnp.sum(upstream, axis=0, keepdims=True)

    tile_lanes = width // 4
    for shard in range(4):
        give[shard] = out_sum[:, shard * tile_lanes : (shard + 1) * tile_lanes]
    small.step(0)
    run([(piece, 2) for piece in second])
    small.step(1)
    run([(query[0], 3), (first[0], 4), (first[1], 4)])
    run([(piece, 3) for piece in second])
    small.step(2)


def back(saved, tok, dres, early, vec, edge, grads):
    qh, kv, mixed, lse, doh = saved
    g_late, g_down, g_vec = grads
    depth = lax.axis_size("grp") // 2
    rows, width = tok.shape
    size, slots = qh.shape[1], rows // 3
    lanes = 2 * size
    whole = (2, 2, depth, 2)
    own_down = g_down.shape[0] // (8 * depth)
    parts = rows // PART
    shapes = [(3, ROWS, width), (2, ROWS, width)] + [(own_down // 2, width)] * 2
    shapes += [(1, ROWS, width)] + [(2, ROWS, width), (1, ROWS, width)] * 2
    ring = pltpu.SemaphoreType.DMA((9 * scatter_slots(depth) + 2 * depth + 2,))
    swaps = pltpu.SemaphoreType.DMA((6 * parts + 7,))
    g_late = g_late.reshape(LATE, *whole, ROWS, width)
    g_down = g_down.reshape(*whole, own_down, width)
    inputs = (tok, kv, doh, qh, mixed, g_late, g_down, early, dres)
    return pl.pallas_call(
        functools.partial(back_kernel, depth),
        out_shape=(
            shaped(rows, width),
            shaped(EARLY, ROWS, width, kind=WIDE),
            shaped(LATE, ROWS, width, kind=WIDE),
            shaped(own_down, width, kind=WIDE),
            shaped(ROWS, width // 4, kind=WIDE),
        ),
        in_specs=[pl.BlockSpec(memory_space=pl.ANY)] * 9 + in_vmem(4),
        out_specs=in_vmem(5),
        scratch_shapes=[
            buf for order, shape in zip(SCATTER_ORDERS, shapes) for buf in scatter_scratch(depth, order, shape)
        ]
        + [pltpu.VMEM(x.shape, x.dtype) for x in inputs]
        + [
            pltpu.VMEM((EARLY, *whole, ROWS, width), LOW),
            pltpu.VMEM(kv.shape, WIDE),
            pltpu.VMEM((2, lanes, 4 * slots), LOW),
            pltpu.VMEM(qh.shape, LOW),
            pltpu.VMEM((2, 4, size, rows), LOW),
            pltpu.VMEM(kv.shape, LOW),
            pltpu.VMEM((2, slots, width), LOW),
            pltpu.VMEM((width // 128, rows + 8, 128), WIDE),
            pltpu.VMEM((rows, width), LOW),
            pltpu.VMEM((width // 128, rows + 8, 128), WIDE),
            pltpu.VMEM((rows, width), WIDE),
            pltpu.VMEM((width // 128, 8, 128), WIDE),
            pltpu.VMEM((5, ROWS, width // 4), WIDE),
            pltpu.VMEM((2 * depth + 2, ROWS, width // 4), WIDE),
            pltpu.VMEM(vec.shape, WIDE),
            ring,
            ring,
            swaps,
            swaps,
            pltpu.SemaphoreType.DMA((9,)),
        ],
        compiler_params=pltpu.CompilerParams(
            collective_id=2, has_side_effects=True, vmem_limit_bytes=62 * MEGA
        ),
    )(*inputs, lse, vec, edge, g_vec)


def update_kernel(*refs):
    weights, firsts, seconds = refs[0:6], refs[6:12], refs[12:18]
    early, late, down, vec = refs[18:22]
    held, outs, passed, kept, sems = refs[22:24], refs[24:48], refs[48:50], refs[50:52], refs[52]
    arriving = [pltpu.make_async_copy(held[k], kept[k], sems.at[k]) for k in range(2)]
    leaving = [pltpu.make_async_copy(kept[k], passed[k], sems.at[2 + k]) for k in range(2)]
    for made in arriving:
        made.start()
    width = early.shape[-1]

    def put(which, at, gradient):
        results = adamw(
            weights[which][at], gradient, firsts[which][at], seconds[which][at], LEARNING_RATES[which]
        )
        for group, value in enumerate(results):
            outs[6 * group + which][at] = value

    every = slice(None)
    put(0, (every, every), early[0])
    for k in range(2):
        arriving[k].wait()
        leaving[k].start()
    size = width // H
    for tap in range(3):
        for kind in range(2):
            columns = [
                early[1 + 3 * half + tap, :, (2 * s + kind) * size : (2 * s + kind + 1) * size]
                for half in range(2)
                for s in range(4)
            ]
            put(1, (tap, every, slice(kind * width, (kind + 1) * width)), jnp.concatenate(columns, axis=1))
    put(2, (every, every), late[0])
    for part in range(4):
        put(3, (every, slice(part * width, (part + 1) * width)), late[1 + part])
    put(4, (every, every), down[...])
    share = weights[5].shape[1]
    tile_lanes = vec.shape[1]
    tile = pltpu.roll(vec[...], lax.rem(tile_lanes - lax.axis_index("grp") * share, tile_lanes), 1)
    put(5, (every, every), tile[0 : weights[5].shape[0], 0:share])
    for made in leaving:
        made.wait()


def update(params, firsts, seconds, grads, held):
    outs = [jax.ShapeDtypeStruct(member.shape, WIDE) for member in params] * 3
    outs += [jax.ShapeDtypeStruct(member.shape, LOW) for member in params]
    return pl.pallas_call(
        update_kernel,
        out_shape=tuple(outs) + tuple(jax.ShapeDtypeStruct(x.shape, x.dtype) for x in held),
        in_specs=in_vmem(22) + [pl.BlockSpec(memory_space=pl.ANY)] * 2,
        out_specs=in_vmem(24) + [pl.BlockSpec(memory_space=pl.ANY)] * 2,
        scratch_shapes=[pltpu.VMEM(x.shape, x.dtype) for x in held] + [pltpu.SemaphoreType.DMA((4,))],
    )(*params, *firsts, *seconds, *grads, *held)


def fused(tokens, cotangent, lengths, *state):
    params, firsts, seconds = state[0:6], state[6:12], state[12:18]
    width = tokens.shape[2]
    tok, cot = tokens[0], cotangent[0]
    early, late, down, vec, edge, qh, kv, mixed, lse, attended = front(tok, params)
    early = early.reshape(EARLY, width, width)
    late = late.reshape(LATE, width, width)
    down = down.reshape(-1, width)
    out, dres, doh, g_late, g_down, g_vec = middle(
        tok, cot, attended, late, down, vec, lengths.reshape(1, 1)
    )
    grad, r_early, r_late, r_down, r_vec = back(
        (qh, kv, mixed, lse, doh), tok, dres, early, vec, edge, (g_late, g_down, g_vec)
    )
    *new, out, grad = update(params, firsts, seconds, (r_early, r_late, r_down, r_vec), (out, grad))
    return (out[None], grad[None], *new)


def body(*arguments):
    tokens, shard = arguments[0], arguments[3]
    whole_tiles = shard.shape[0] % ROWS == 0 and tokens.shape[1] % PART == 0
    four = lax.axis_size("seq") == 4 and lax.axis_size("grp") % 2 == 0
    return (fused if whole_tiles and four else plain)(*arguments)


def solution(mesh):
    in_specs = (
        P("grp", "seq", None),
        P("grp", "seq", None),
        P("grp"),
        P(("seq", "grp"), None),
        P(None, ("seq", "grp"), None),
        P(("seq", "grp"), None),
        P(("seq", "grp"), None),
        P(("seq", "grp"), None),
        P(None, ("seq", "grp")),
        P(("seq", "grp"), None),
        P(None, ("seq", "grp"), None),
        P(("seq", "grp"), None),
        P(("seq", "grp"), None),
        P(("seq", "grp"), None),
        P(None, ("seq", "grp")),
        P(("seq", "grp"), None),
        P(None, ("seq", "grp"), None),
        P(("seq", "grp"), None),
        P(("seq", "grp"), None),
        P(("seq", "grp"), None),
        P(None, ("seq", "grp")),
    )
    out_specs = (
        P("grp", "seq", None),
        P("grp", "seq", None),
        P(("seq", "grp"), None),
        P(None, ("seq", "grp"), None),
        P(("seq", "grp"), None),
        P(("seq", "grp"), None),
        P(("seq", "grp"), None),
        P(None, ("seq", "grp")),
        P(("seq", "grp"), None),
        P(None, ("seq", "grp"), None),
        P(("seq", "grp"), None),
        P(("seq", "grp"), None),
        P(("seq", "grp"), None),
        P(None, ("seq", "grp")),
        P(("seq", "grp"), None),
        P(None, ("seq", "grp"), None),
        P(("seq", "grp"), None),
        P(("seq", "grp"), None),
        P(("seq", "grp"), None),
        P(None, ("seq", "grp")),
        P(("seq", "grp"), None),
        P(None, ("seq", "grp"), None),
        P(("seq", "grp"), None),
        P(("seq", "grp"), None),
        P(("seq", "grp"), None),
        P(None, ("seq", "grp")),
    )
    return jax.shard_map(body, mesh=mesh, in_specs=in_specs, out_specs=out_specs, check_vma=False)
```

profile of v0, /device:TPU:0, one launch (start us, length us, event | category | flops | bytes accessed | tf_op | source)
XLA Modules:
  0.0 202.4 jit_solution(6512709150235481795)
XLA Ops:
  1.3 81.4 %shard_map.404 = (bf16[7,2,2,4,2,16,512]{6,5,4,3,2,1,0:T(8,128)(2,1)}, bf16[5,2,2,4,2,16,512]{6,5,4,3,2,1,0:T(8,128)(2,1)}, bf16[2,2,4,2,64,512]{5,4,3,2,1,0:T(8...) custom-call(bf16[1152,512]{1,0:T(8,128)(2,1)} %bitcast.11, ...), custom_call_target="tpu_custom_call" | custom-call | tf_op jit(solution)/shard_map/pallas_call | solution.py:968
  82.7 29.4 %shard_map.405 = (bf16[1152,512]{1,0:T(8,128)(2,1)}, f32[1152,512]{1,0:T(8,128)}, bf16[2,64,4608]{2,1,0:T(8,128)(2,1)}, bf16[5,512,512]{2,1,0:T(8,128)(2,1)}, bf...) custom-call(bf16[1152,512]{1,0:T(8,128)(2,1)} %bitcast.12, bf16[1152,512]{1,0:T(8,128)(2,1)} %bitcast.19, ...), custom_call_target="tpu_custom_call" | custom-call | tf_op jit(solution)/shard_map/pallas_call | solution.py:1135
  112.1 84.3 %shard_map.406 = (bf16[1152,512]{1,0:T(8,128)(2,1)}, f32[7,16,512]{2,1,0:T(8,128)}, f32[5,16,512]{2,1,0:T(8,128)}, f32[64,512]{1,0:T(8,128)}, f32[16,128]{1,0:T(8,128)}) custom-call(bf16[1152,512]{1,0:T(8,128)(2,1)} %bitcast.13, bf16[2,1536,128]{2,1,0:T(8,128)(2,1)} %get-tuple-element.73.refs_1_, bf16[2,64,4608]{2,1,0:T(8,128)(2,1)} %get-tuple-element.78.refs_2_, ...), custom_call_target="tpu_custom_call" | custom-call | tf_op jit(solution)/shard_map/pallas_call | solution.py:1452
  196.4 5.7 %shard_map.407 = (f32[16,512]{1,0:T(8,128)}, f32[3,16,1024]{2,1,0:T(8,128)}, f32[16,512]{1,0:T(8,128)}, f32[16,2048]{1,0:T(8,128)}, f32[64,512]{1,0:T(8,128)}, /...) custom-call(f32[16,512]{1,0:T(8,128)} %refs_0_.1, ...), custom_call_target="tpu_custom_call" | custom-call | tf_op jit(solution)/shard_map/pallas_call | solution.py:1541
where the time goes:
time: 205 us; the launch traced here: 202 us
  Pallas kernels  201 us (98%)
    pallas_call x1, Pallas kernels, back(): pl.pallas_call(functools.partial(back_kernel, depth), out_shape=(shaped(r...  84.3 us
    pallas_call x1, Pallas kernels, front(): pl.pallas_call(functools.partial(front_kernel, depth), out_shape=(shaped(...  81.4 us
    pallas_call x1, Pallas kernels, middle(): pl.pallas_call(functools.partial(middle_kernel, lax.axis_size('grp') // 2...  29.4 us
    pallas_call x1, Pallas kernels, update(): pl.pallas_call(update_kernel, out_shape=tuple(outs) + tuple((jax.ShapeDty...  5.71 us

commit v1 on v0

--- a/solution.py
+++ b/solution.py
@@ -1363,10 +1363,10 @@
     put_early(0, dot(turned, low_a[...]).T)
     query[0].step(0)
     da[...] = lax.dot_general(turned.T, early[0], NT, preferred_element_type=WIDE)
-    query[0].step(1)
-    run([(piece, 2) for piece in first])
     for turn in (1, 2, 3):
         memory_copy(1, turn).wait()
+    run([(piece, 2) for piece in first])
+    query[0].step(1)
     for tap in range(3):
         memory_gradient(1, tap)
         if tap:
@@ -1387,7 +1387,6 @@
         edge_copy().start()
 
     run([(piece, 1) for piece in second])
-    run([(piece, 4) for piece in soon])
     run([(query[0], 2), (first[0], 3), (first[1], 3)])
 
     @pl.when(p.seq < 3)
@@ -1426,6 +1425,7 @@
         give[shard] = out_sum[:, shard * tile_lanes : (shard + 1) * tile_lanes]
     small.step(0)
     run([(piece, 2) for piece in second])
+    run([(piece, 4) for piece in soon])
     small.step(1)
     run([(query[0], 3), (first[0], 4), (first[1], 4)])
     run([(piece, 3) for piece in second])
@@ -1495,11 +1495,9 @@
 def update_kernel(*refs):
     weights, firsts, seconds = refs[0:6], refs[6:12], refs[12:18]
     early, late, down, vec = refs[18:22]
-    held, outs, passed, kept, sems = refs[22:24], refs[24:48], refs[48:50], refs[50:52], refs[52]
-    arriving = [pltpu.make_async_copy(held[k], kept[k], sems.at[k]) for k in range(2)]
-    leaving = [pltpu.make_async_copy(kept[k], passed[k], sems.at[2 + k]) for k in range(2)]
-    for made in arriving:
-        made.start()
+    held, outs, passed = refs[22:24], refs[24:48], refs[48:50]
+    for source, target in zip(held, passed):
+        target[...] = source[...]
     width = early.shape[-1]
 
     def put(which, at, gradient):
@@ -1511,9 +1509,6 @@
 
     every = slice(None)
     put(0, (every, every), early[0])
-    for k in range(2):
-        arriving[k].wait()
-        leaving[k].start()
     size = width // H
     for tap in range(3):
         for kind in range(2):
@@ -1531,8 +1526,6 @@
     tile_lanes = vec.shape[1]
     tile = pltpu.roll(vec[...], lax.rem(tile_lanes - lax.axis_index("grp") * share, tile_lanes), 1)
     put(5, (every, every), tile[0 : weights[5].shape[0], 0:share])
-    for made in leaving:
-        made.wait()
 
 
 def update(params, firsts, seconds, grads, held):
@@ -1541,9 +1534,8 @@
     return pl.pallas_call(
         update_kernel,
         out_shape=tuple(outs) + tuple(jax.ShapeDtypeStruct(x.shape, x.dtype) for x in held),
-        in_specs=in_vmem(22) + [pl.BlockSpec(memory_space=pl.ANY)] * 2,
-        out_specs=in_vmem(24) + [pl.BlockSpec(memory_space=pl.ANY)] * 2,
-        scratch_shapes=[pltpu.VMEM(x.shape, x.dtype) for x in held] + [pltpu.SemaphoreType.DMA((4,))],
+        in_specs=in_vmem(24),
+        out_specs=in_vmem(26),
     )(*params, *firsts, *seconds, *grads, *held)
 
 

time: 205 us -> 203 us (level)
  no operation moved by 1% of the time
where the time goes in v1:
time: 203 us; the launch traced here: 200 us
  Pallas kernels  199 us (98%)
    pallas_call x1, Pallas kernels, back(): pl.pallas_call(functools.partial(back_kernel, depth), out_shape=(shaped(r...  83.1 us
    pallas_call x1, Pallas kernels, front(): pl.pallas_call(functools.partial(front_kernel, depth), out_shape=(shaped(...  81.4 us
    pallas_call x1, Pallas kernels, middle(): pl.pallas_call(functools.partial(middle_kernel, lax.axis_size('grp') // 2...  29.4 us
    pallas_call x1, Pallas kernels, update(): pl.pallas_call(update_kernel, out_shape=tuple(outs) + tuple((jax.ShapeDty...  4.8 us

profile of v1, /device:TPU:0, one launch (start us, length us, event | category | flops | bytes accessed | tf_op | source)
XLA Modules:
  0.0 200.2 jit_solution(13328808944229940508)
XLA Ops:
  1.3 81.4 %shard_map.404 = (bf16[7,2,2,4,2,16,512]{6,5,4,3,2,1,0:T(8,128)(2,1)}, bf16[5,2,2,4,2,16,512]{6,5,4,3,2,1,0:T(8,128)(2,1)}, bf16[2,2,4,2,64,512]{5,4,3,2,1,0:T(8...) custom-call(bf16[1152,512]{1,0:T(8,128)(2,1)} %bitcast.11, ...), custom_call_target="tpu_custom_call" | custom-call | tf_op jit(solution)/shard_map/pallas_call | solution.py:968
  82.7 29.4 %shard_map.405 = (bf16[1152,512]{1,0:T(8,128)(2,1)}, f32[1152,512]{1,0:T(8,128)}, bf16[2,64,4608]{2,1,0:T(8,128)(2,1)}, bf16[5,512,512]{2,1,0:T(8,128)(2,1)}, bf...) custom-call(bf16[1152,512]{1,0:T(8,128)(2,1)} %bitcast.12, bf16[1152,512]{1,0:T(8,128)(2,1)} %bitcast.19, ...), custom_call_target="tpu_custom_call" | custom-call | tf_op jit(solution)/shard_map/pallas_call | solution.py:1135
  112.1 83.1 %shard_map.406 = (bf16[1152,512]{1,0:T(8,128)(2,1)}, f32[7,16,512]{2,1,0:T(8,128)}, f32[5,16,512]{2,1,0:T(8,128)}, f32[64,512]{1,0:T(8,128)}, f32[16,128]{1,0:T(8,128)}) custom-call(bf16[1152,512]{1,0:T(8,128)(2,1)} %bitcast.13, bf16[2,1536,128]{2,1,0:T(8,128)(2,1)} %get-tuple-element.73.refs_1_, bf16[2,64,4608]{2,1,0:T(8,128)(2,1)} %get-tuple-element.78.refs_2_, ...), custom_call_target="tpu_custom_call" | custom-call | tf_op jit(solution)/shard_map/pallas_call | solution.py:1452
  195.2 4.8 %shard_map.407 = (f32[16,512]{1,0:T(8,128)}, f32[3,16,1024]{2,1,0:T(8,128)}, f32[16,512]{1,0:T(8,128)}, f32[16,2048]{1,0:T(8,128)}, f32[64,512]{1,0:T(8,128)}, /...) custom-call(f32[16,512]{1,0:T(8,128)} %refs_0_.1, ...), custom_call_target="tpu_custom_call" | custom-call | tf_op jit(solution)/shard_map/pallas_call | solution.py:1534

commit v2 on v1

--- a/solution.py
+++ b/solution.py
@@ -792,10 +792,10 @@
         piece.step(1)
     for piece in soon:
         piece.step(3)
+    for piece in soon:
+        piece.step(4)
     for piece in later[:1] + later[3:]:
         piece.step(2)
-    for piece in soon:
-        piece.step(4)
 
     @pl.when(p.seq > 0)
     def _():
@@ -1049,7 +1049,7 @@
         )
         return [pltpu.make_async_copy(a, b, osem.at[3 * number + k]) for k, (a, b) in enumerate(pairs)]
 
-    for made in arriving:
+    for made in arriving[:3]:
         made.wait()
 
     @pl.loop(0, parts)
@@ -1061,6 +1061,11 @@
         unit, factor = unit_rows_of(residual)
         normed = (unit * gain + shift).astype(LOW)
         cs[here, :] = normed
+        @pl.when(number == 0)
+        def _():
+            for k, (source, target) in ((3, (down_in, down)), (4, (cot_in, cot))):
+                pltpu.make_async_copy(source, target, isem.at[k]).wait()
+
         place = lax.broadcasted_iota(jnp.int32, (PART, 1), 0) + (p.seq * rows + at)
         live = (place < length[0, 0]).astype(WIDE)
         upstream = cot[here, :].astype(WIDE) * live
@@ -1307,7 +1312,7 @@
         def _():
             send_memory(0)
 
-        @pl.when(turn_number == strips + 2)
+        @pl.when(turn_number == strips + 3)
         def _():
             for turn in (1, 2, 3):
                 memory_copy(0, turn).wait()
@@ -1344,7 +1349,7 @@
         for when, steps in (
             (1, [(piece, 1) for piece in soon]),
             (7, [(piece, 2) for piece in soon]),
-            (9, [(piece, 1) for piece in first]),
+            (10, [(piece, 1) for piece in first]),
             (10, [(piece, 3) for piece in soon]),
         ):
 

time: 203 us -> 202 us (level)
  no operation moved by 1% of the time
where the time goes in v2:
time: 202 us; the launch traced here: 199 us
  Pallas kernels  198 us (98%)
    pallas_call x1, Pallas kernels, back(): pl.pallas_call(functools.partial(back_kernel, depth), out_shape=(shaped(r...  82.4 us
    pallas_call x1, Pallas kernels, front(): pl.pallas_call(functools.partial(front_kernel, depth), out_shape=(shaped(...  81.4 us
    pallas_call x1, Pallas kernels, middle(): pl.pallas_call(functools.partial(middle_kernel, lax.axis_size('grp') // 2...  29 us
    pallas_call x1, Pallas kernels, update(): pl.pallas_call(update_kernel, out_shape=tuple(outs) + tuple((jax.ShapeDty...  4.8 us

profile of v2, /device:TPU:0, one launch (start us, length us, event | category | flops | bytes accessed | tf_op | source)
XLA Modules:
  0.0 199.2 jit_solution(3750833293125809178)
XLA Ops:
  1.3 81.4 %shard_map.404 = (bf16[7,2,2,4,2,16,512]{6,5,4,3,2,1,0:T(8,128)(2,1)}, bf16[5,2,2,4,2,16,512]{6,5,4,3,2,1,0:T(8,128)(2,1)}, bf16[2,2,4,2,64,512]{5,4,3,2,1,0:T(8...) custom-call(bf16[1152,512]{1,0:T(8,128)(2,1)} %bitcast.11, ...), custom_call_target="tpu_custom_call" | custom-call | tf_op jit(solution)/shard_map/pallas_call | solution.py:968
  82.7 29.0 %shard_map.405 = (bf16[1152,512]{1,0:T(8,128)(2,1)}, f32[1152,512]{1,0:T(8,128)}, bf16[2,64,4608]{2,1,0:T(8,128)(2,1)}, bf16[5,512,512]{2,1,0:T(8,128)(2,1)}, bf...) custom-call(bf16[1152,512]{1,0:T(8,128)(2,1)} %bitcast.12, bf16[1152,512]{1,0:T(8,128)(2,1)} %bitcast.19, ...), custom_call_target="tpu_custom_call" | custom-call | tf_op jit(solution)/shard_map/pallas_call | solution.py:1140
  111.8 82.4 %shard_map.406 = (bf16[1152,512]{1,0:T(8,128)(2,1)}, f32[7,16,512]{2,1,0:T(8,128)}, f32[5,16,512]{2,1,0:T(8,128)}, f32[64,512]{1,0:T(8,128)}, f32[16,128]{1,0:T(8,128)}) custom-call(bf16[1152,512]{1,0:T(8,128)(2,1)} %bitcast.13, bf16[2,1536,128]{2,1,0:T(8,128)(2,1)} %get-tuple-element.73.refs_1_, bf16[2,64,4608]{2,1,0:T(8,128)(2,1)} %get-tuple-element.78.refs_2_, ...), custom_call_target="tpu_custom_call" | custom-call | tf_op jit(solution)/shard_map/pallas_call | solution.py:1457
  194.1 4.8 %shard_map.407 = (f32[16,512]{1,0:T(8,128)}, f32[3,16,1024]{2,1,0:T(8,128)}, f32[16,512]{1,0:T(8,128)}, f32[16,2048]{1,0:T(8,128)}, f32[64,512]{1,0:T(8,128)}, /...) custom-call(f32[16,512]{1,0:T(8,128)} %refs_0_.1, ...), custom_call_target="tpu_custom_call" | custom-call | tf_op jit(solution)/shard_map/pallas_call | solution.py:1539
